TPU v7x, 32 devices: a whole 2x2x4 slice. The times are simulated.
32 devices in a mesh: rad: 8 (over z, x), az: 4 (over y, core).
Axes of the slice: x: 2, y: 2, z: 4, core: 2. Of those that a mesh axis runs over, the one named last changes fastest.
Arguments:
- state: float32 [6, 2, 256, 4096], P(None, None, 'rad', 'az'), may hold values from -4 to 4, as said below
- offsets: int32 [256], P('rad'), may hold values from 0 to 4095
- viscosity: float32 [2, 256, 4096], P(None, 'rad', 'az'), may hold values from 0.02 to 0.2
- absorb: float32 [2, 256, 4096], P(None, 'rad', 'az'), may hold values from 0.5 to 8
Outputs:
- new_state: float32 [6, 2, 256, 4096], P(None, None, 'rad', 'az')
- depth: float32 [2, 256, 4096], P(None, 'rad', 'az')
Inputs may be any that keep to these rules, and one draw needn't show every extreme that they name: state[0] lies in 0.5 to 2, state[1], state[2], state[3] in -4 to 4, state[4] in 1 to 3, state[5] in 0.1 to 1.
All inputs are finite; a program needn't handle non-finite values.
Results may differ from a plain program's by a relative error of at most 0.00002.
Values sent between devices are 32-bit elements; how exact they have to be, the bound alone decides.
A program may use at most 128 MiB of HBM per device.

v0:
```python
import jax
import jax.numpy as jnp
from jax import lax
from jax.sharding import PartitionSpec as P

AZIMUTH_COEF = 0.1


def shifted_2(block, axis, distance):
    devices = range(lax.axis_size(axis))
    route = [((i - distance) % len(devices), i) for i in devices]
    return lax.ppermute(block, axis, route)


def padded(block, sides, width, periodic):
    for axis, dim in sides:
        count = lax.axis_size(axis)
        forward = [(i, i + 1) for i in range(count - 1)]
        if periodic:
            forward.append((count - 1, 0))
        backward = [(target, source) for source, target in forward]
        low = lax.ppermute(
            lax.slice_in_dim(block, block.shape[dim] - width, None, axis=dim), axis, forward
        )
        high = lax.ppermute(lax.slice_in_dim(block, 0, width, axis=dim), axis, backward)
        block = jnp.concatenate([low, block, high], axis=dim)
    return block


def entering(value, axis, join, neutral):
    count, mine = (lax.axis_size(axis), lax.axis_index(axis))
    pieces = lax.all_gather(value, axis)
    subtotal = jnp.full_like(value, 0) + jnp.asarray(neutral, value.dtype)

    def turn(position, subtotal):
        longer = join(subtotal, pieces[position])
        return jnp.where(position < mine, longer, subtotal)

    return lax.fori_loop(0, count - 1, turn, subtotal)


def add_depth(earlier, later):
    return earlier + later


def body(state, offsets, viscosity, absorb):
    n_azimuth = lax.axis_size("az")
    n_radial = lax.axis_size("rad")
    width = state.shape[3]
    radial_cells = state.shape[2]
    before = shifted_2(state, "az", 1)
    extended = jnp.concatenate([before, state], axis=3)
    remainder = offsets % width
    whole_moves = offsets // width

    def slide_row(row_block, amount):
        return lax.dynamic_slice_in_dim(row_block, width - amount, width, axis=2)

    shifted = jax.vmap(slide_row, in_axes=(2, 0), out_axes=2)(extended, remainder)
    for bit_index in range((n_azimuth - 1).bit_length()):
        arrived = shifted_2(shifted, "az", 1 << bit_index)
        selected = whole_moves >> bit_index & 1 == 1
        shifted = jnp.where(selected[None, None, :, None], arrived, shifted)
    radial_pad = padded(shifted, (("rad", 2),), 1, False)
    azimuth_pad = padded(shifted, (("az", 3),), 1, True)
    radial_term = radial_pad[:, :, 2:] + radial_pad[:, :, :-2] - 2.0 * shifted
    azimuth_term = azimuth_pad[:, :, :, 2:] + azimuth_pad[:, :, :, :-2] - 2.0 * shifted
    smoothed = shifted + viscosity[None] * radial_term + AZIMUTH_COEF * azimuth_term
    total_radial = radial_cells * n_radial
    depth_step = 2.0 * absorb * smoothed[5] / total_radial
    local_depth = jnp.cumsum(depth_step, axis=1)
    column_total = local_depth[:, -1, :]
    carried = entering(column_total, "rad", add_depth, jnp.zeros_like(column_total))
    depth = carried[:, None, :] + local_depth - 0.5 * depth_step
    radius = (lax.axis_index("rad") * radial_cells + jnp.arange(radial_cells)).astype(
        jnp.float32
    ) + 0.5
    stellar_flux = 1.0 / (1.0 + radius / total_radial)
    energy = smoothed[4] + stellar_flux[None, :, None] * jnp.exp(-depth)
    new_state = jnp.concatenate([smoothed[:4], energy[None], smoothed[5:]], axis=0)
    return (new_state, depth)


def solution(mesh):
    in_specs = (P(None, None, "rad", "az"), P("rad"), P(None, "rad", "az"), P(None, "rad", "az"))
    out_specs = (P(None, None, "rad", "az"), P(None, "rad", "az"))
    return jax.shard_map(body, mesh=mesh, in_specs=in_specs, out_specs=out_specs, check_vma=False)
```

profile of v0, /device:TPU:0, one launch (start us, length us, event | category | flops | bytes accessed | tf_op | source)
XLA Modules:
  0.0 246.1 jit_solution(16927806639478889778)
XLA Ops:
  0.6 2.6 %copy.9 = f32[6,2,32,1024]{3,1,0,2:T(2,128)S(1)} copy(f32[6,2,32,1024]{3,2,1,0:T(8,128)} %param.6) | data formatting | bytes 3145728 | tf_op args[0]
  3.8 20.1 %collective-permute-done = f32[6,2,32,1024]{3,1,0,2:T(2,128)} collective-permute-done((f32[6,2,32,1024]{3,1,0,2:T(2,128)S(1)}, f32[6,2,32,1024]{3,1,0,2:T(2,128)}, u32[]{:S(2)}, u32[]{:S(2)}) %collective-permute-start) | collective-permute-done | bytes 1572896 | tf_op jit(solution)/shard_map/ppermute | solution.py:12
  23.9 5.0 %maximum_bitcast_fusion = f32[32,6,2,2048]{3,2,1,0:T(2,128)} fusion(f32[6,2,32,1024]{3,1,0,2:T(2,128)S(1)} %copy.9, f32[6,2,32,1024]{3,1,0,2:T(2,128)} %collective-permute-done), kind=kLoop, calls=%fused_computation.3 | loop fusion | flops 786432 | bytes 6291456 | tf_op jit(solution)/shard_map/vmap()/transpose | solution.py:57
  28.9 110.1 %while.15 = (s32[]{:T(128)}, f32[32,6,2,2048]{3,2,1,0:T(2,128)}, s32[32,4]{0,1:T(4,128)S(1)}, f32[32,6,2,1024]{3,0,2,1:T(8,128)S(1)}, s32[]{:T(128)}, /*index=5*/s32[]{:T(128)}) while((s32[]{:T(128)}, f32[32,6,2,2048]{3,2,1,0:T(2,128)}, s32[32,4]{0,1:T(4,128)S(1)}, f32[32,6,2,1024]{3,0,2,1:T(8,128)S(1)}, s32[]{:T(128)}, /*index=5*/s32[]{:T(128)}) %tuple.54), condition=%wide.while_cond, body=%wide.while_body.sunk | while | flops 2 | bytes 295045 | solution.py:57
  29.5 2.2 constant_dynamic-slice_fusion.5
  33.0 2.2 constant_dynamic-slice_fusion.5
  36.4 2.2 constant_dynamic-slice_fusion.5
  39.9 2.2 constant_dynamic-slice_fusion.5
  43.3 2.2 constant_dynamic-slice_fusion.5
  46.8 2.2 constant_dynamic-slice_fusion.5
  50.2 2.2 constant_dynamic-slice_fusion.5
  53.6 2.2 constant_dynamic-slice_fusion.5
  57.1 2.2 constant_dynamic-slice_fusion.5
  60.5 2.2 constant_dynamic-slice_fusion.5
  64.0 2.2 constant_dynamic-slice_fusion.5
  67.4 2.2 constant_dynamic-slice_fusion.5
  70.8 2.2 constant_dynamic-slice_fusion.5
  74.3 2.2 constant_dynamic-slice_fusion.5
  77.7 2.2 constant_dynamic-slice_fusion.5
  81.2 2.2 constant_dynamic-slice_fusion.5
  84.6 2.2 constant_dynamic-slice_fusion.5
  88.1 2.2 constant_dynamic-slice_fusion.5
  91.5 2.2 constant_dynamic-slice_fusion.5
  94.9 2.2 constant_dynamic-slice_fusion.5
  98.4 2.2 constant_dynamic-slice_fusion.5
  101.8 2.2 constant_dynamic-slice_fusion.5
  105.3 2.2 constant_dynamic-slice_fusion.5
  108.7 2.2 constant_dynamic-slice_fusion.5
  112.2 2.2 constant_dynamic-slice_fusion.5
  115.6 2.2 constant_dynamic-slice_fusion.5
  119.0 2.2 constant_dynamic-slice_fusion.5
  122.5 2.2 constant_dynamic-slice_fusion.5
  125.9 2.2 constant_dynamic-slice_fusion.5
  129.4 2.2 constant_dynamic-slice_fusion.5
  132.8 2.2 constant_dynamic-slice_fusion.5
  136.2 2.2 constant_dynamic-slice_fusion.5
  139.2 19.8 %collective-permute-done.1 = f32[6,2,32,1024]{3,2,1,0:T(8,128)S(1)} collective-permute-done((f32[6,2,32,1024]{3,2,1,0:T(8,128)S(1)}, f32[6,2,32,1024]{3,2,1,0:T(8,128)S(1)}, u32[]{:S(2)}, u32[]{:S(2)}) %collective-permute-start.1) | collective-permute-done | bytes 1572896 | tf_op jit(solution)/shard_map/ppermute | solution.py:12
  159.3 2.4 collective-permute-start.2
  161.7 34.0 %collective-permute-done.2 = f32[6,2,32,1024]{3,2,1,0:T(8,128)} collective-permute-done((f32[6,2,32,1024]{3,2,1,0:T(8,128)S(1)}, f32[6,2,32,1024]{3,2,1,0:T(8,128)}, u32[]{:S(2)}, u32[]{:S(2)}) %collective-permute-start.2) | collective-permute-done | bytes 1572896 | tf_op jit(solution)/shard_map/ppermute | solution.py:12
  195.7 1.8 broadcast_select_fusion.1
  198.3 1.3 collective-permute-start.3
  199.6 4.5 %collective-permute-start.4 = (f32[6,2,1,1024]{3,2,1,0:T(1,128)S(1)}, f32[6,2,1,1024]{3,2,1,0:T(1,128)S(1)}, u32[]{:S(2)}, u32[]{:S(2)}) collective-permute-start(f32[6,2,1,1024]{3,2,1,0:T(1,128)S(1)} %get-tuple-element.128), channel_id=1, source_target_pairs={{0,4},{4,8},{8,12},{12,16},{16,20},{20,24},{24,28},{1,5},{5,9},{9,... | collective-permute-start | bytes 147464 | tf_op jit(solution)/shard_map/ppermute | solution.py:22
  204.9 1.0 collective-permute-done.4
  205.9 2.1 fusion.3
  208.1 0.8 copy-done
  209.2 33.4 %all-gather = f32[16,1,1024]{2,1,0:T(1,128)S(1)} all-gather(f32[2,1,1024]{2,1,0:T(1,128)S(1)} %slice.78), channel_id=2, replica_groups=mesh['rad'=8,'az'=4] {'rad'}, dimensions={0}, use_global_device_ids=true | all-gather | bytes 73728 | tf_op jit(solution)/shard_map/all_gather | solution.py:32
  243.1 1.7 fusion.9
  244.9 1.2 pad_maximum_fusion.4
  (168 shorter events, 41.7 us)
Async XLA Ops:
  0.6 3.1 %copy-start.3 = (s32[32]{0:T(128)S(1)}, s32[32]{0:T(128)}, u32[]{:S(2)}) copy-start(s32[32]{0:T(128)} %param.7) | copy-start | bytes 388
  3.3 20.7 %collective-permute-start = (f32[6,2,32,1024]{3,1,0,2:T(2,128)S(1)}, f32[6,2,32,1024]{3,1,0,2:T(2,128)}, u32[]{:S(2)}, u32[]{:S(2)}) collective-permute-start(f32[6,2,32,1024]{3,1,0,2:T(2,128)S(1)} %copy.9), channel_id=1, source_target_pairs={{3,0},{0,1},{1,2},{2,3},{7,4},{4,5},{5,6},{6,7},{11,8},{8,9},{9,10... | collective-permute-start | bytes 4718600 | tf_op jit(solution)/shard_map/ppermute | solution.py:12
  139.1 19.9 %collective-permute-start.1 = (f32[6,2,32,1024]{3,2,1,0:T(8,128)S(1)}, f32[6,2,32,1024]{3,2,1,0:T(8,128)S(1)}, u32[]{:S(2)}, u32[]{:S(2)}) collective-permute-start(f32[6,2,32,1024]{3,2,1,0:T(8,128)S(1)} %bitcast.31), channel_id=1, source_target_pairs={{3,0},{0,1},{1,2},{2,3},{7,4},{4,5},{5,6},{6,7},{11,8},{8,9},{9,10... | collective-permute-start | bytes 4718600 | tf_op jit(solution)/shard_map/ppermute | solution.py:12
  159.3 36.4 %collective-permute-start.2 = (f32[6,2,32,1024]{3,2,1,0:T(8,128)S(1)}, f32[6,2,32,1024]{3,2,1,0:T(8,128)}, u32[]{:S(2)}, u32[]{:S(2)}) collective-permute-start(f32[6,2,32,1024]{3,2,1,0:T(8,128)S(1)} %broadcast_select_fusion), channel_id=1, source_target_pairs={{2,0},{3,1},{0,2},{1,3},{6,4},{7,5},{4,6},{5,7},{10,8},{11,9},{8,1... | collective-permute-start | bytes 4718600 | tf_op jit(solution)/shard_map/ppermute | solution.py:12
  195.7 10.1 %copy-start.1 = (f32[2,32,1024]{2,1,0:T(8,128)S(1)}, f32[2,32,1024]{2,1,0:T(8,128)}, u32[]{:S(2)}) copy-start(f32[2,32,1024]{2,1,0:T(8,128)} %param.8) | copy-start | bytes 786436
  197.7 6.4 %collective-permute-start.5 = (f32[6,2,32,1]{3,2,1,0:T(8,128)S(1)}, f32[6,2,32,1]{3,2,1,0:T(8,128)}, u32[]{:S(2)}, u32[]{:S(2)}) collective-permute-start(f32[6,2,32,1]{3,2,1,0:T(8,128)S(1)} %get-tuple-element.129), channel_id=1, source_target_pairs={{1,0},{2,1},{3,2},{0,3},{5,4},{6,5},{7,6},{4,7},{9,8},{10,9},{11,1... | collective-permute-start | bytes 4616 | tf_op jit(solution)/shard_map/ppermute | solution.py:25
  197.8 6.4 %collective-permute-start.6 = (f32[6,2,32,1]{3,2,1,0:T(8,128)S(1)}, f32[6,2,32,1]{3,2,1,0:T(8,128)S(1)}, u32[]{:S(2)}, u32[]{:S(2)}) collective-permute-start(f32[6,2,32,1]{3,2,1,0:T(8,128)S(1)} %get-tuple-element.130), channel_id=1, source_target_pairs={{0,1},{1,2},{2,3},{3,0},{4,5},{5,6},{6,7},{7,4},{8,9},{9,10},{10,1... | collective-permute-start | bytes 4616 | tf_op jit(solution)/shard_map/ppermute | solution.py:22
  198.3 6.0 %collective-permute-start.3 = (f32[6,2,1,1024]{3,2,1,0:T(1,128)S(1)}, f32[6,2,1,1024]{3,2,1,0:T(1,128)S(1)}, u32[]{:S(2)}, u32[]{:S(2)}) collective-permute-start(f32[6,2,1,1024]{3,2,1,0:T(1,128)S(1)} %get-tuple-element.127), channel_id=1, source_target_pairs={{4,0},{8,4},{12,8},{16,12},{20,16},{24,20},{28,24},{5,1},{9,5},{13... | collective-permute-start | bytes 147464 | tf_op jit(solution)/shard_map/ppermute | solution.py:25
  199.6 6.3 %collective-permute-start.4 = (f32[6,2,1,1024]{3,2,1,0:T(1,128)S(1)}, f32[6,2,1,1024]{3,2,1,0:T(1,128)S(1)}, u32[]{:S(2)}, u32[]{:S(2)}) collective-permute-start(f32[6,2,1,1024]{3,2,1,0:T(1,128)S(1)} %get-tuple-element.128), channel_id=1, source_target_pairs={{0,4},{4,8},{8,12},{12,16},{16,20},{20,24},{24,28},{1,5},{5,9},{9,... | collective-permute-start | bytes 147464 | tf_op jit(solution)/shard_map/ppermute | solution.py:22
  204.2 0.7 copy-start.2
  208.0 1.0 copy-start
where the time goes:
time: 249 us; the launch traced here: 246 us
  local copies, waits for them, and re-layouts  113 us (45%)
  waiting for transfers between devices  75 us (30%)
  blocking collectives  33.4 us (13%)
  other arithmetic  12.8 us (5%)
  starting transfers between devices  9.31 us (4%)
    gather x160, local copies, waits for them, and re-layouts  109 us
    ppermute x3, waiting for transfers between devices, shifted_2(): return lax.ppermute(block, axis, route)  74 us
    all_gather x1, blocking collectives, entering(): pieces = lax.all_gather(value, axis)  33.4 us
    ppermute x2, starting transfers between devices, padded(): lax.ppermute(lax.slice_in_dim(block, block.shape[dim] - width, None, axis...  5.04 us
    transpose x1, other arithmetic, slide_row(): return lax.dynamic_slice_in_dim(row_block, width - amount, width, axis=2)  4.99 us
  transfers between devices with their start and end apart: 7, of which 5 were waited for; matrix products, arithmetic and copies ran while one was open for 0% of the time, Pallas kernels for 0%

commit v1 on v0

v1 whole, which is shorter than its diff:
```python
import functools

import jax
import jax.numpy as jnp
from jax import lax
from jax.experimental import pallas as pl
from jax.experimental.pallas import tpu as pltpu
from jax.sharding import PartitionSpec as P

AZIMUTH_COEF = 0.1
LANES = 128
SUB = 8


def kernel(n_rad, n_az, state, offs, visc, absorb, out, depth, buf, sh, eo, ei, tot_out, tot_in, ss, rs):
    groups = n_az // 2
    rad = lax.axis_index("rad")
    az = lax.axis_index("az")
    core = lax.rem(az, 2)
    sibling = {"az": az + 1 - 2 * core}
    planes, rows, width = state.shape
    cols = width // LANES
    tiles = rows // SUB
    dust = planes - 2
    rest = dust
    total_rows = rows * n_rad

    def rad_at(k):
        return {"rad": lax.rem(rad + k + n_rad, n_rad)}

    def az_at(k):
        return {"az": lax.rem(az + 2 * k, n_az)}

    count = [0]

    def remote(src, dst, device):
        i = count[0]
        count[0] += 1
        return pltpu.make_async_remote_copy(
            src_ref=src, dst_ref=dst, send_sem=ss.at[i], recv_sem=rs.at[i],
            device_id=device, device_id_type=pl.DeviceIdType.MESH,
        )

    peers = [az_at(k) for k in range(1, groups)] + [sibling] + [rad_at(k) for k in range(1, n_rad)]
    barrier = pltpu.get_barrier_semaphore()
    for peer in peers:
        pl.semaphore_signal(barrier, inc=1, device_id=peer, device_id_type=pl.DeviceIdType.MESH)
    pl.semaphore_wait(barrier, len(peers))

    pieces = [(dust, 2, 0, rows)]
    edge_tiles = [0, tiles - 1]
    for t in edge_tiles + list(range(1, tiles - 2)):
        pieces.append((0, rest, t * SUB, SUB))
    half = rest // 2
    pieces.append((0, half, (tiles - 2) * SUB, SUB))
    pieces.append((half, rest - half, (tiles - 2) * SUB, SUB))

    sent = []
    across, beside = [], []
    for p0, np_, r0, nr in pieces:
        ps, rws = pl.ds(p0, np_), pl.ds(r0, nr)
        across.append([remote(state.at[ps, rws], buf.at[2 * k - 1, ps, rws], az_at(k)) for k in range(1, groups)])
        beside.append(remote(state.at[ps, rws], buf.at[0, ps, rws], sibling))
        for c in across[-1] + [beside[-1]]:
            c.start()
            sent.append(c)

    def arrive(i):
        p0, np_, r0, nr = pieces[i]
        ps, rws = pl.ds(p0, np_), pl.ds(r0, nr)
        forwards = []
        for k in range(1, groups):
            across[i][k - 1].wait_recv()
            f = remote(buf.at[2 * k - 1, ps, rws], buf.at[2 * k, ps, rws], sibling)
            f.start()
            sent.append(f)
            forwards.append(f)
        beside[i].wait_recv()
        for f in forwards:
            f.wait_recv()

    lane = lax.broadcasted_iota(jnp.int32, (SUB, LANES), 1)

    def shift_tile(tile, p0, np_):
        r = pl.ds(tile * SUB, SUB)
        amount = offs[r, :]
        block = amount // width
        within = amount - block * width
        column = within // LANES
        rem = within - column * LANES
        pick = (lane - rem) & (LANES - 1)
        low = lane < rem

        def one(p, carry):
            def load(d, c):
                cs = pl.ds(c * LANES, LANES)
                if d == 0:
                    return state[p, r, cs]
                if d % 2 == 0:
                    return buf[d - 1, p, r, cs]
                slot = jnp.where(core == 1, d, (d + 2) % n_az)
                return buf[slot - 1, p, r, cs]

            line = []
            for move, c in [(1, c) for c in range(cols)] + [(0, c) for c in range(cols)] + [(-1, 0)]:
                value = load(move % n_az, c)
                for b in range(1, n_az):
                    value = jnp.where(block == b, load((b + move) % n_az, c), value)
                line.append(value)
            step = cols // 2
            while step:
                chosen = (column & step) != 0
                line = [jnp.where(chosen, line[i - step], line[i]) for i in range(step, len(line))]
                step //= 2
            turned = [jnp.take_along_axis(v, pick, axis=1, mode="promise_in_bounds") for v in line]
            x = [turned[0]] + [jnp.where(low, turned[j - 1], turned[j]) for j in range(1, len(turned))]
            right = [pltpu.roll(v, 1, 1) for v in x[:-1]]
            left = [pltpu.roll(v, LANES - 1, 1) for v in x[1:]]
            for c in range(cols):
                cs = pl.ds(c * LANES, LANES)
                mid = x[c + 1]
                prev = jnp.where(lane == 0, right[c], right[c + 1])
                nxt = jnp.where(lane == LANES - 1, left[c + 1], left[c])
                sh[p, pl.ds(SUB + tile * SUB, SUB), cs] = mid
                out[p, r, cs] = mid + AZIMUTH_COEF * (nxt + prev - 2.0 * mid)
                if tile == 0:
                    eo[0, p, :, cs] = mid[:1]
                if tile == tiles - 1:
                    eo[1, p, :, cs] = mid[SUB - 1:]
            return carry

        lax.fori_loop(p0, p0 + np_, one, 0)

    def send_edge(side, p0, np_):
        ps = pl.ds(p0, np_)
        c = remote(eo.at[side, ps], ei.at[1 - side, ps], rad_at(-1 if side == 0 else 1))
        c.start()
        sent.append(c)
        return c

    def place_edges(p0, np_):
        def one(p, carry):
            sh[p, SUB - 1:SUB, :] = jnp.where(rad > 0, ei[0, p], 0.0)
            sh[p, SUB + rows:SUB + rows + 1, :] = jnp.where(rad < n_rad - 1, ei[1, p], 0.0)
            return carry

        lax.fori_loop(p0, p0 + np_, one, 0)

    def smooth(tile, p0, np_):
        top = SUB + tile * SUB

        def one(p, carry):
            r = pl.ds(tile * SUB, SUB)
            mid = sh[p, top:top + SUB, :]
            up = sh[p, top - 1:top + SUB - 1, :]
            down = sh[p, top + 1:top + SUB + 1, :]
            out[p, r, :] = out[p, r, :] + visc[lax.rem(p, 2), r, :] * (down + up - 2.0 * mid)
            return carry

        lax.fori_loop(p0, p0 + np_, one, 0)

    arrive(0)
    for t in range(tiles):
        shift_tile(t, dust, 2)
    edges = [send_edge(s, dust, 2) for s in (0, 1)]
    for e in edges:
        e.wait_recv()
    place_edges(dust, 2)
    for t in range(tiles):
        smooth(t, dust, 2)

    row = lax.broadcasted_iota(jnp.int32, (SUB, width), 0)
    for h in range(2):
        base = jnp.zeros((1, width), jnp.float32)
        for t in range(tiles):
            r = pl.ds(t * SUB, SUB)
            step = 2.0 * absorb[h, r, :] * out[dust + h, r, :] / total_rows
            run = step
            for k in (1, 2, 4):
                run = run + jnp.where(row >= k, pltpu.roll(run, k, 0), 0.0)
            run = run + base
            depth[h, r, :] = run - 0.5 * step
            base = run[SUB - 1:]
        tot_out[h] = base
    totals = []
    for k in range(1, n_rad):
        c = remote(tot_out, tot_in.at[k - 1], rad_at(k))
        c.start()
        sent.append(c)
        totals.append(c)

    arrive(1)
    shift_tile(0, 0, rest)
    edge_in = send_edge(0, 0, rest)
    arrive(2)
    shift_tile(tiles - 1, 0, rest)
    edge_out = send_edge(1, 0, rest)

    for c in totals:
        c.wait_recv()
    for h in range(2):
        carried = jnp.zeros((1, width), jnp.float32)
        for k in range(1, n_rad):
            carried = carried + jnp.where(k <= rad, tot_in[k - 1, h], 0.0)
        for t in range(tiles):
            r = pl.ds(t * SUB, SUB)
            depth[h, r, :] = depth[h, r, :] + carried

    edge_in.wait_recv()
    edge_out.wait_recv()
    place_edges(0, rest)
    i = 3
    for t in range(1, tiles - 2):
        arrive(i)
        shift_tile(t, 0, rest)
        smooth(t - 1, 0, rest)
        i += 1

    def last(p0, np_):
        shift_tile(tiles - 2, p0, np_)
        for t in range(max(tiles - 3, 0), tiles):
            smooth(t, p0, np_)

    arrive(i)
    last(0, half)
    arrive(i + 1)
    last(half, rest - half)
    for h in range(2):
        for t in range(tiles):
            r = pl.ds(t * SUB, SUB)
            radius = (rad * rows + t * SUB + row).astype(jnp.float32) + 0.5
            flux = 1.0 / (1.0 + radius / total_rows)
            out[rest - 2 + h, r, :] = out[rest - 2 + h, r, :] + flux * jnp.exp(-depth[h, r, :])
    for c in sent:
        c.wait_send()


def body(n_rad, n_az, state, offsets, viscosity, absorb):
    fields, polar, rows, width = state.shape
    planes = fields * polar
    groups = n_az // 2
    tiles = rows // SUB
    n_pieces = 1 + 2 + max(tiles - 3, 0) + 2
    n_sems = n_pieces * (2 * (groups - 1) + 1) + 4 + n_rad - 1
    offs = jnp.broadcast_to(offsets[:, None], (rows, LANES))
    f32 = jnp.float32
    vm = pl.BlockSpec(memory_space=pltpu.VMEM)
    new_state, depth = pl.pallas_call(
        functools.partial(kernel, n_rad, n_az),
        out_shape=(
            jax.ShapeDtypeStruct((planes, rows, width), f32),
            jax.ShapeDtypeStruct((polar, rows, width), f32),
        ),
        in_specs=[vm] * 4,
        out_specs=(vm, vm),
        scratch_shapes=[
            pltpu.VMEM((n_az - 1, planes, rows, width), f32),
            pltpu.VMEM((planes, rows + 2 * SUB, width), f32),
            pltpu.VMEM((2, planes, 1, width), f32),
            pltpu.VMEM((2, planes, 1, width), f32),
            pltpu.VMEM((polar, 1, width), f32),
            pltpu.VMEM((n_rad - 1, polar, 1, width), f32),
            pltpu.SemaphoreType.DMA((n_sems,)),
            pltpu.SemaphoreType.DMA((n_sems,)),
        ],
        compiler_params=pltpu.CompilerParams(
            collective_id=0, has_side_effects=True, vmem_limit_bytes=56 * 2**20
        ),
    )(state.reshape(planes, rows, width), offs, viscosity, absorb)
    return new_state.reshape(state.shape), depth


def solution(mesh):
    in_specs = (P(None, None, "rad", "az"), P("rad"), P(None, "rad", "az"), P(None, "rad", "az"))
    out_specs = (P(None, None, "rad", "az"), P(None, "rad", "az"))
    f = functools.partial(body, mesh.shape["rad"], mesh.shape["az"])
    return jax.shard_map(f, mesh=mesh, in_specs=in_specs, out_specs=out_specs, check_vma=False)
```

time: 249 us -> 52.9 us (0.21); the launches traced: 246 us -> 52.8 us
  local copies, waits for them, and re-layouts: 113 us -> 4.81 us
  waiting for transfers between devices: 75 us -> 0 us
  Pallas kernels: 0 us -> 47.3 us
  blocking collectives: 33.4 us -> 0 us
  other arithmetic: 12.8 us -> 0 us
  starting transfers between devices: 9.31 us -> 0 us
    gather x160 -> x0, local copies, waits for them, and re-layouts: 109 us -> none
    ppermute x7 -> x0, waiting for transfers between devices: 75 us -> none  [the longest x3 74 us: shifted_2(): return lax.ppermute(block, axis, route)]
    pallas_call x0 -> x1, Pallas kernels: none -> 47.3 us  [body(): pl.pallas_call(functools.partial(kernel, n_rad, n_az), out_shape=(jax.Sha...]
    all_gather x1 -> x0, blocking collectives: 33.4 us -> none  [entering(): pieces = lax.all_gather(value, axis)]
    ppermute x7 -> x0, starting transfers between devices: 9.31 us -> none  [the longest x2 5.04 us: padded(): lax.ppermute(lax.slice_in_dim(block, block.shape[dim] - width, None, axis...]
    transpose x1 -> x0, other arithmetic: 4.99 us -> none  [slide_row(): return lax.dynamic_slice_in_dim(row_block, width - amount, width, axis=2)]
  transfers between devices with their start and end apart: 7 -> 0, of which waited for: 5 -> 0; matrix products, arithmetic and copies ran while one was open for 0% -> 0% of each run, Pallas kernels for 0% -> 0%
where the time goes in v1:
time: 52.9 us; the launch traced here: 52.8 us
  Pallas kernels  47.3 us (89%)
  local copies, waits for them, and re-layouts  4.81 us (9%)
  between operations  0.65 us (1%)
    pallas_call x1, Pallas kernels, body(): pl.pallas_call(functools.partial(kernel, n_rad, n_az), out_shape=(jax.Sha...  47.3 us
    unnamed x4, local copies, waits for them, and re-layouts  3.48 us
    broadcast_in_dim x1, local copies, waits for them, and re-layouts, body(): offs = jnp.broadcast_to(offsets[:, None], (rows, LANES))  1.33 us

profile of v1, /device:TPU:0, one launch (start us, length us, event | category | flops | bytes accessed | tf_op | source)
XLA Modules:
  0.0 52.8 jit_solution(3507124721297208777)
XLA Ops:
  0.6 1.3 %broadcast_in_dim.2.offs = s32[32,128]{1,0:T(8,128)} broadcast(s32[32]{0:T(128)} %param.5), dimensions={0} | broadcast | bytes 16512 | tf_op jit(solution)/shard_map/broadcast_in_dim | solution.py:245
  2.0 47.3 %shard_map.59 = (f32[12,32,1024]{2,1,0:T(8,128)}, f32[2,32,1024]{2,1,0:T(8,128)}) custom-call(f32[12,32,1024]{2,1,0:T(8,128)} %bitcast.3, s32[32,128]{1,0:T(8,128)} %broadcast_in_dim.2.offs, f32[2,32,1024]{2,1,0:T(8,128)} %visc.1, f32[2,32,1024]{2,1,0:T(8,128)} %absorb.1), custom_call_target="tpu_custom_call" | custom-call | tf_op jit(solution)/shard_map/pallas_call | solution.py:248
  49.3 0.0 copy-start
  49.3 2.8 %copy.8 = f32[6,2,32,1024]{3,2,1,0:T(8,128)} copy(f32[6,2,32,1024]{3,2,1,0:T(8,128)} %bitcast.2) | data formatting | bytes 3145728
  52.1 0.0 copy-done
  52.1 0.7 %copy.9 = f32[2,32,1024]{2,1,0:T(8,128)} copy(f32[2,32,1024]{2,1,0:T(8,128)S(1)} %copy-done) | data formatting | bytes 524288
Async XLA Ops:
  49.3 2.8 %copy-start = (f32[2,32,1024]{2,1,0:T(8,128)S(1)}, f32[2,32,1024]{2,1,0:T(8,128)}, u32[]{:S(2)}) copy-start(f32[2,32,1024]{2,1,0:T(8,128)} %get-tuple-element.9) | copy-start | bytes 786436

commit v2 on v1

--- a/solution.py
+++ b/solution.py
@@ -12,7 +12,13 @@
 SUB = 8
 
 
-def kernel(n_rad, n_az, state, offs, visc, absorb, out, depth, buf, sh, eo, ei, tot_out, tot_in, ss, rs):
+def tail_planes(rest):
+    cuts = [0, rest * 4 // 10, rest * 7 // 10, rest * 9 // 10, rest]
+    return [(a, b - a) for a, b in zip(cuts, cuts[1:]) if b > a]
+
+
+def kernel(n_rad, n_az, source, offs, visc, absorb, result, depth, carry_out, heat,
+           state, out, buf, sh, eo, ei, tot_out, tot_in, ss, rs, ls):
     groups = n_az // 2
     rad = lax.axis_index("rad")
     az = lax.axis_index("az")
@@ -41,6 +47,16 @@
             device_id=device, device_id_type=pl.DeviceIdType.MESH,
         )
 
+    fetch = pltpu.make_async_copy(source, state, ls.at[0])
+    fetch.start()
+    stored = []
+
+    def store(p0, np_, r0, nr):
+        at = (pl.ds(p0, np_), pl.ds(r0, nr))
+        c = pltpu.make_async_copy(out.at[at], result.at[at], ls.at[1 + len(stored)])
+        c.start()
+        stored.append(c)
+
     peers = [az_at(k) for k in range(1, groups)] + [sibling] + [rad_at(k) for k in range(1, n_rad)]
     barrier = pltpu.get_barrier_semaphore()
     for peer in peers:
@@ -51,16 +67,16 @@
     edge_tiles = [0, tiles - 1]
     for t in edge_tiles + list(range(1, tiles - 2)):
         pieces.append((0, rest, t * SUB, SUB))
-    half = rest // 2
-    pieces.append((0, half, (tiles - 2) * SUB, SUB))
-    pieces.append((half, rest - half, (tiles - 2) * SUB, SUB))
+    tail = tail_planes(rest)
+    for p0, np_ in tail:
+        pieces.append((p0, np_, (tiles - 2) * SUB, SUB))
 
     sent = []
     across, beside = [], []
     for p0, np_, r0, nr in pieces:
         ps, rws = pl.ds(p0, np_), pl.ds(r0, nr)
-        across.append([remote(state.at[ps, rws], buf.at[2 * k - 1, ps, rws], az_at(k)) for k in range(1, groups)])
-        beside.append(remote(state.at[ps, rws], buf.at[0, ps, rws], sibling))
+        across.append([remote(source.at[ps, rws], buf.at[2 * k - 1, ps, rws], az_at(k)) for k in range(1, groups)])
+        beside.append(remote(source.at[ps, rws], buf.at[0, ps, rws], sibling))
         for c in across[-1] + [beside[-1]]:
             c.start()
             sent.append(c)
@@ -83,7 +99,10 @@
 
     def shift_tile(tile, p0, np_):
         r = pl.ds(tile * SUB, SUB)
-        amount = offs[r, :]
+        sub = lax.broadcasted_iota(jnp.int32, (SUB, LANES), 0)
+        amount = jnp.full((SUB, LANES), offs[tile * SUB], jnp.int32)
+        for k in range(1, SUB):
+            amount = jnp.where(sub == k, offs[tile * SUB + k], amount)
         block = amount // width
         within = amount - block * width
         column = within // LANES
@@ -160,6 +179,7 @@
         lax.fori_loop(p0, p0 + np_, one, 0)
 
     arrive(0)
+    fetch.wait()
     for t in range(tiles):
         shift_tile(t, dust, 2)
     edges = [send_edge(s, dust, 2) for s in (0, 1)]
@@ -168,6 +188,7 @@
     place_edges(dust, 2)
     for t in range(tiles):
         smooth(t, dust, 2)
+    store(dust, 2, 0, rows)
 
     row = lax.broadcasted_iota(jnp.int32, (SUB, width), 0)
     for h in range(2):
@@ -202,9 +223,12 @@
         carried = jnp.zeros((1, width), jnp.float32)
         for k in range(1, n_rad):
             carried = carried + jnp.where(k <= rad, tot_in[k - 1, h], 0.0)
+        carry_out[h:h + 1, :] = carried
         for t in range(tiles):
             r = pl.ds(t * SUB, SUB)
-            depth[h, r, :] = depth[h, r, :] + carried
+            radius = (rad * rows + t * SUB + row).astype(jnp.float32) + 0.5
+            flux = 1.0 / (1.0 + radius / total_rows)
+            heat[h, r, :] = flux * jnp.exp(-(depth[h, r, :] + carried))
 
     edge_in.wait_recv()
     edge_out.wait_recv()
@@ -214,23 +238,18 @@
         arrive(i)
         shift_tile(t, 0, rest)
         smooth(t - 1, 0, rest)
+        store(0, rest, (t - 1) * SUB, SUB)
         i += 1
-
-    def last(p0, np_):
+    first = max(tiles - 3, 0)
+    for p0, np_ in tail:
+        arrive(i)
         shift_tile(tiles - 2, p0, np_)
-        for t in range(max(tiles - 3, 0), tiles):
+        for t in range(first, tiles):
             smooth(t, p0, np_)
-
-    arrive(i)
-    last(0, half)
-    arrive(i + 1)
-    last(half, rest - half)
-    for h in range(2):
-        for t in range(tiles):
-            r = pl.ds(t * SUB, SUB)
-            radius = (rad * rows + t * SUB + row).astype(jnp.float32) + 0.5
-            flux = 1.0 / (1.0 + radius / total_rows)
-            out[rest - 2 + h, r, :] = out[rest - 2 + h, r, :] + flux * jnp.exp(-depth[h, r, :])
+        store(p0, np_, first * SUB, (tiles - first) * SUB)
+        i += 1
+    for c in stored:
+        c.wait()
     for c in sent:
         c.wait_send()
 
@@ -240,20 +259,25 @@
     planes = fields * polar
     groups = n_az // 2
     tiles = rows // SUB
-    n_pieces = 1 + 2 + max(tiles - 3, 0) + 2
+    n_tail = len(tail_planes(planes - 2))
+    n_pieces = 1 + 2 + max(tiles - 3, 0) + n_tail
     n_sems = n_pieces * (2 * (groups - 1) + 1) + 4 + n_rad - 1
-    offs = jnp.broadcast_to(offsets[:, None], (rows, LANES))
     f32 = jnp.float32
     vm = pl.BlockSpec(memory_space=pltpu.VMEM)
-    new_state, depth = pl.pallas_call(
+    hbm = pl.BlockSpec(memory_space=pl.ANY)
+    moved, local, carried, heat = pl.pallas_call(
         functools.partial(kernel, n_rad, n_az),
         out_shape=(
             jax.ShapeDtypeStruct((planes, rows, width), f32),
             jax.ShapeDtypeStruct((polar, rows, width), f32),
+            jax.ShapeDtypeStruct((polar, width), f32),
+            jax.ShapeDtypeStruct((polar, rows, width), f32),
         ),
-        in_specs=[vm] * 4,
-        out_specs=(vm, vm),
+        in_specs=[hbm, pl.BlockSpec(memory_space=pltpu.SMEM), vm, vm],
+        out_specs=(hbm, vm, vm, vm),
         scratch_shapes=[
+            pltpu.VMEM((planes, rows, width), f32),
+            pltpu.VMEM((planes, rows, width), f32),
             pltpu.VMEM((n_az - 1, planes, rows, width), f32),
             pltpu.VMEM((planes, rows + 2 * SUB, width), f32),
             pltpu.VMEM((2, planes, 1, width), f32),
@@ -262,12 +286,15 @@
             pltpu.VMEM((n_rad - 1, polar, 1, width), f32),
             pltpu.SemaphoreType.DMA((n_sems,)),
             pltpu.SemaphoreType.DMA((n_sems,)),
+            pltpu.SemaphoreType.DMA((2 + max(tiles - 3, 0) + n_tail,)),
         ],
         compiler_params=pltpu.CompilerParams(
             collective_id=0, has_side_effects=True, vmem_limit_bytes=56 * 2**20
         ),
-    )(state.reshape(planes, rows, width), offs, viscosity, absorb)
-    return new_state.reshape(state.shape), depth
+    )(state.reshape(planes, rows, width), offsets, viscosity, absorb)
+    moved = moved.reshape(state.shape)
+    field = lax.broadcasted_iota(jnp.int32, state.shape, 0)
+    return jnp.where(field == fields - 2, moved + heat[None], moved), local + carried[:, None, :]
 
 
 def solution(mesh):

time: 52.9 us -> 54.4 us (1.028)
  local copies, waits for them, and re-layouts: 4.81 us -> 0 us
  other arithmetic: 0 us -> 4.71 us
  Pallas kernels: 47.3 us -> 48.5 us
    unnamed x4 -> x0, local copies, waits for them, and re-layouts: 3.48 us -> none
    select_n x0 -> x1, other arithmetic: none -> 3.02 us  [body(): jnp.where(field == fields - 2, moved + heat[None], moved)]
    add x0 -> x1, other arithmetic: none -> 1.68 us  [body(): local + carried[:, None, :]]
    broadcast_in_dim x1 -> x0, local copies, waits for them, and re-layouts: 1.33 us -> none  [body(): offs = jnp.broadcast_to(offsets[:, None], (rows, LANES))]
    pallas_call x1, Pallas kernels: 47.3 us -> 48.5 us  [body(): pl.pallas_call(functools.partial(kernel, n_rad, n_az), out_shape=(jax.Sha...]
where the time goes in v2:
time: 54.4 us; the launch traced here: 53.9 us
  Pallas kernels  48.5 us (89%)
  other arithmetic  4.71 us (9%)
  between operations  0.64 us (1%)
    pallas_call x1, Pallas kernels, body(): pl.pallas_call(functools.partial(kernel, n_rad, n_az), out_shape=(jax.Sha...  48.5 us
    select_n x1, other arithmetic, body(): jnp.where(field == fields - 2, moved + heat[None], moved)  3.02 us
    add x1, other arithmetic, body(): local + carried[:, None, :]  1.68 us

profile of v2, /device:TPU:0, one launch (start us, length us, event | category | flops | bytes accessed | tf_op | source)
XLA Modules:
  0.0 53.9 jit_solution(10068804772034775555)
XLA Ops:
  0.6 48.5 %shard_map.59 = (f32[12,32,1024]{2,1,0:T(8,128)}, f32[2,32,1024]{2,1,0:T(8,128)}, f32[2,1024]{1,0:T(2,128)}, f32[2,32,1024]{2,1,0:T(8,128)}) custom-call(f32[12,32,1024]{2,1,0:T(8,128)} %bitcast.2, s32[32]{0:T(128)} %offs.1, f32[2,32,1024]{2,1,0:T(8,128)} %visc.1, f32[2,32,1024]{2,1,0:T(8,128)} %absorb.1), custom_call_target="tpu_custom_call" | custom-call | tf_op jit(solution)/shard_map/pallas_call | solution.py:268
  49.2 1.7 %broadcast_add_fusion = f32[2,32,1024]{2,1,0:T(8,128)} fusion(f32[2,32,1024]{2,1,0:T(8,128)} %get-tuple-element.8, f32[2,1024]{1,0:T(2,128)} %get-tuple-element.9), kind=kLoop, calls=%fused_computation.1 | loop fusion | flops 65536 | bytes 532480 | tf_op jit(solution)/shard_map/add | solution.py:297
  50.9 3.0 %add_select_fusion = f32[6,2,32,1024]{3,2,1,0:T(8,128)} fusion(f32[6,2,32,1024]{3,2,1,0:T(8,128)} %bitcast.3, f32[2,32,1024]{2,1,0:T(8,128)} %get-tuple-element.7, pred[6]{0:T(512)(128)(4,1)S(1)} %iota_compare_fusion), kind=kLoop, calls=%fused_computation | loop fusion | flops 786432 | bytes 3407878 | tf_op jit(solution)/shard_map/jit(_where)/select_n | solution.py:297
  (1 shorter events, 0.0 us)

commit v3 on v2

--- a/solution.py
+++ b/solution.py
@@ -13,12 +13,12 @@
 
 
 def tail_planes(rest):
-    cuts = [0, rest * 4 // 10, rest * 7 // 10, rest * 9 // 10, rest]
+    cuts = [0, rest // 2, rest]
     return [(a, b - a) for a, b in zip(cuts, cuts[1:]) if b > a]
 
 
-def kernel(n_rad, n_az, source, offs, visc, absorb, result, depth, carry_out, heat,
-           state, out, buf, sh, eo, ei, tot_out, tot_in, ss, rs, ls):
+def kernel(n_rad, n_az, source, offs, visc, absorb, result, depth,
+           heat, state, out, buf, sh, eo, ei, tot_out, tot_in, ss, rs, ls):
     groups = n_az // 2
     rad = lax.axis_index("rad")
     az = lax.axis_index("az")
@@ -57,11 +57,27 @@
         c.start()
         stored.append(c)
 
-    peers = [az_at(k) for k in range(1, groups)] + [sibling] + [rad_at(k) for k in range(1, n_rad)]
+    inner, outer = rad > 0, rad < n_rad - 1
+    ei[...] = jnp.zeros_like(ei)
+    tot_in[...] = jnp.zeros_like(tot_in)
+    peers = [az_at(k) for k in range(1, groups)] + [sibling]
     barrier = pltpu.get_barrier_semaphore()
+    for there, k in ((inner, -1), (outer, 1)):
+        @pl.when(there)
+        def _():
+            pl.semaphore_signal(barrier, inc=1, device_id=rad_at(k), device_id_type=pl.DeviceIdType.MESH)
     for peer in peers:
         pl.semaphore_signal(barrier, inc=1, device_id=peer, device_id_type=pl.DeviceIdType.MESH)
-    pl.semaphore_wait(barrier, len(peers))
+    senders = len(peers)
+    d = 1
+    while d < n_rad:
+        if d > 1:
+            @pl.when(rad >= d)
+            def _():
+                pl.semaphore_signal(barrier, inc=1, device_id=rad_at(-d), device_id_type=pl.DeviceIdType.MESH)
+            senders = senders + (rad + d < n_rad).astype(jnp.int32)
+        d *= 2
+    pl.semaphore_wait(barrier, senders + inner.astype(jnp.int32) + outer.astype(jnp.int32))
 
     pieces = [(dust, 2, 0, rows)]
     edge_tiles = [0, tiles - 1]
@@ -71,7 +87,7 @@
     for p0, np_ in tail:
         pieces.append((p0, np_, (tiles - 2) * SUB, SUB))
 
-    sent = []
+    sent, chained = [], []
     across, beside = [], []
     for p0, np_, r0, nr in pieces:
         ps, rws = pl.ds(p0, np_), pl.ds(r0, nr)
@@ -150,12 +166,33 @@
 
         lax.fori_loop(p0, p0 + np_, one, 0)
 
+    hops = []
+
+    def scan_send():
+        i = len(hops)
+        d = 1 << i
+        if d < n_rad:
+            c = remote(tot_out.at[i], tot_in.at[i], rad_at(d))
+            goes = rad + d < n_rad
+            pl.when(goes)(c.start)
+            chained.append((goes, c))
+            hops.append(c)
+
+    def scan_take():
+        i = len(hops) - 1
+        pl.when(rad >= 1 << i)(hops[i].wait_recv)
+        tot_out[i + 1] = tot_out[i] + tot_in[i]
+
     def send_edge(side, p0, np_):
         ps = pl.ds(p0, np_)
         c = remote(eo.at[side, ps], ei.at[1 - side, ps], rad_at(-1 if side == 0 else 1))
-        c.start()
-        sent.append(c)
-        return c
+        goes, comes = (inner, outer) if side == 0 else (outer, inner)
+        pl.when(goes)(c.start)
+        chained.append((goes, c))
+        return comes, c
+
+    def edge_wait(edge):
+        pl.when(edge[0])(edge[1].wait_recv)
 
     def place_edges(p0, np_):
         def one(p, carry):
@@ -184,7 +221,7 @@
         shift_tile(t, dust, 2)
     edges = [send_edge(s, dust, 2) for s in (0, 1)]
     for e in edges:
-        e.wait_recv()
+        edge_wait(e)
     place_edges(dust, 2)
     for t in range(tiles):
         smooth(t, dust, 2)
@@ -202,42 +239,46 @@
             run = run + base
             depth[h, r, :] = run - 0.5 * step
             base = run[SUB - 1:]
-        tot_out[h] = base
-    totals = []
-    for k in range(1, n_rad):
-        c = remote(tot_out, tot_in.at[k - 1], rad_at(k))
-        c.start()
-        sent.append(c)
-        totals.append(c)
-
+        tot_out[0, h] = base
+    scan_send()
     arrive(1)
     shift_tile(0, 0, rest)
     edge_in = send_edge(0, 0, rest)
+    scan_take()
+    scan_send()
     arrive(2)
     shift_tile(tiles - 1, 0, rest)
     edge_out = send_edge(1, 0, rest)
 
-    for c in totals:
-        c.wait_recv()
+    scan_take()
+    while 1 << len(hops) < n_rad:
+        scan_send()
+        scan_take()
     for h in range(2):
-        carried = jnp.zeros((1, width), jnp.float32)
-        for k in range(1, n_rad):
-            carried = carried + jnp.where(k <= rad, tot_in[k - 1, h], 0.0)
-        carry_out[h:h + 1, :] = carried
+        carried = tot_in[0, h]
+        for i in range(1, len(hops)):
+            carried = carried + tot_in[i, h]
         for t in range(tiles):
             r = pl.ds(t * SUB, SUB)
             radius = (rad * rows + t * SUB + row).astype(jnp.float32) + 0.5
             flux = 1.0 / (1.0 + radius / total_rows)
-            heat[h, r, :] = flux * jnp.exp(-(depth[h, r, :] + carried))
-
-    edge_in.wait_recv()
-    edge_out.wait_recv()
+            depth[h, r, :] = depth[h, r, :] + carried
+            heat[h, r, :] = flux * jnp.exp(-depth[h, r, :])
+
+    def warm(tile):
+        r = pl.ds(tile * SUB, SUB)
+        for h in range(2):
+            out[rest - 2 + h, r, :] = out[rest - 2 + h, r, :] + heat[h, r, :]
+
+    edge_wait(edge_in)
+    edge_wait(edge_out)
     place_edges(0, rest)
     i = 3
     for t in range(1, tiles - 2):
         arrive(i)
         shift_tile(t, 0, rest)
         smooth(t - 1, 0, rest)
+        warm(t - 1)
         store(0, rest, (t - 1) * SUB, SUB)
         i += 1
     first = max(tiles - 3, 0)
@@ -246,10 +287,14 @@
         shift_tile(tiles - 2, p0, np_)
         for t in range(first, tiles):
             smooth(t, p0, np_)
+            if p0 + np_ == rest:
+                warm(t)
         store(p0, np_, first * SUB, (tiles - first) * SUB)
         i += 1
     for c in stored:
         c.wait()
+    for goes, c in chained:
+        pl.when(goes)(c.wait_send)
     for c in sent:
         c.wait_send()
 
@@ -261,29 +306,29 @@
     tiles = rows // SUB
     n_tail = len(tail_planes(planes - 2))
     n_pieces = 1 + 2 + max(tiles - 3, 0) + n_tail
-    n_sems = n_pieces * (2 * (groups - 1) + 1) + 4 + n_rad - 1
+    n_scan = (n_rad - 1).bit_length()
+    n_sems = n_pieces * (2 * (groups - 1) + 1) + 4 + n_scan
     f32 = jnp.float32
     vm = pl.BlockSpec(memory_space=pltpu.VMEM)
     hbm = pl.BlockSpec(memory_space=pl.ANY)
-    moved, local, carried, heat = pl.pallas_call(
+    moved, local = pl.pallas_call(
         functools.partial(kernel, n_rad, n_az),
         out_shape=(
             jax.ShapeDtypeStruct((planes, rows, width), f32),
             jax.ShapeDtypeStruct((polar, rows, width), f32),
-            jax.ShapeDtypeStruct((polar, width), f32),
-            jax.ShapeDtypeStruct((polar, rows, width), f32),
         ),
         in_specs=[hbm, pl.BlockSpec(memory_space=pltpu.SMEM), vm, vm],
-        out_specs=(hbm, vm, vm, vm),
+        out_specs=(hbm, vm),
         scratch_shapes=[
+            pltpu.VMEM((polar, rows, width), f32),
             pltpu.VMEM((planes, rows, width), f32),
             pltpu.VMEM((planes, rows, width), f32),
             pltpu.VMEM((n_az - 1, planes, rows, width), f32),
             pltpu.VMEM((planes, rows + 2 * SUB, width), f32),
             pltpu.VMEM((2, planes, 1, width), f32),
             pltpu.VMEM((2, planes, 1, width), f32),
-            pltpu.VMEM((polar, 1, width), f32),
-            pltpu.VMEM((n_rad - 1, polar, 1, width), f32),
+            pltpu.VMEM((n_scan + 1, polar, 1, width), f32),
+            pltpu.VMEM((n_scan, polar, 1, width), f32),
             pltpu.SemaphoreType.DMA((n_sems,)),
             pltpu.SemaphoreType.DMA((n_sems,)),
             pltpu.SemaphoreType.DMA((2 + max(tiles - 3, 0) + n_tail,)),
@@ -293,8 +338,7 @@
         ),
     )(state.reshape(planes, rows, width), offsets, viscosity, absorb)
     moved = moved.reshape(state.shape)
-    field = lax.broadcasted_iota(jnp.int32, state.shape, 0)
-    return jnp.where(field == fields - 2, moved + heat[None], moved), local + carried[:, None, :]
+    return moved, local
 
 
 def solution(mesh):

time: 54.4 us -> 49.7 us (0.914)
  other arithmetic: 4.71 us -> 0 us
  local copies, waits for them, and re-layouts: 0 us -> 3.48 us
  Pallas kernels: 48.5 us -> 45.4 us
    unnamed x0 -> x4, local copies, waits for them, and re-layouts: none -> 3.48 us
    pallas_call x1, Pallas kernels: 48.5 us -> 45.4 us  [body(): pl.pallas_call(functools.partial(kernel, n_rad, n_az), out_shape=(jax.Sha...]
    select_n x1 -> x0, other arithmetic: 3.02 us -> none  [body(): jnp.where(field == fields - 2, moved + heat[None], moved)]
    add x1 -> x0, other arithmetic: 1.68 us -> none  [body(): local + carried[:, None, :]]
where the time goes in v3:
time: 49.7 us; the launch traced here: 49.5 us
  Pallas kernels  45.4 us (91%)
  local copies, waits for them, and re-layouts  3.48 us (7%)
  between operations  0.65 us (1%)
    pallas_call x1, Pallas kernels, body(): pl.pallas_call(functools.partial(kernel, n_rad, n_az), out_shape=(jax.Sha...  45.4 us
    unnamed x4, local copies, waits for them, and re-layouts  3.48 us

profile of v3, /device:TPU:0, one launch (start us, length us, event | category | flops | bytes accessed | tf_op | source)
XLA Modules:
  0.0 49.5 jit_solution(8412898142860395338)
XLA Ops:
  0.6 45.4 %shard_map.59 = (f32[12,32,1024]{2,1,0:T(8,128)}, f32[2,32,1024]{2,1,0:T(8,128)}) custom-call(f32[12,32,1024]{2,1,0:T(8,128)} %bitcast.2, s32[32]{0:T(128)} %offs.1, f32[2,32,1024]{2,1,0:T(8,128)} %visc.1, f32[2,32,1024]{2,1,0:T(8,128)} %absorb.1), custom_call_target="tpu_custom_call" | custom-call | tf_op jit(solution)/shard_map/pallas_call | solution.py:314
  46.1 0.0 copy-start
  46.1 2.8 %copy.8 = f32[6,2,32,1024]{3,2,1,0:T(8,128)} copy(f32[6,2,32,1024]{3,2,1,0:T(8,128)} %bitcast.3) | data formatting | bytes 3145728
  48.8 0.0 copy-done
  48.8 0.7 %copy.9 = f32[2,32,1024]{2,1,0:T(8,128)} copy(f32[2,32,1024]{2,1,0:T(8,128)S(1)} %copy-done) | data formatting | bytes 524288
Async XLA Ops:
  46.1 2.8 %copy-start = (f32[2,32,1024]{2,1,0:T(8,128)S(1)}, f32[2,32,1024]{2,1,0:T(8,128)}, u32[]{:S(2)}) copy-start(f32[2,32,1024]{2,1,0:T(8,128)} %get-tuple-element.9) | copy-start | bytes 786436

commit v4 on v3

--- a/solution.py
+++ b/solution.py
@@ -17,8 +17,8 @@
     return [(a, b - a) for a, b in zip(cuts, cuts[1:]) if b > a]
 
 
-def kernel(n_rad, n_az, source, offs, visc, absorb, result, depth,
-           heat, state, out, buf, sh, eo, ei, tot_out, tot_in, ss, rs, ls):
+def kernel(n_rad, n_az, n_local, source, offs, visc_in, absorb_in, result, depth,
+           visc, absorb, heat, state, out, buf, sh, eo, ei, tot_out, tot_in, ss, rs, ls):
     groups = n_az // 2
     rad = lax.axis_index("rad")
     az = lax.axis_index("az")
@@ -48,7 +48,10 @@
         )
 
     fetch = pltpu.make_async_copy(source, state, ls.at[0])
-    fetch.start()
+    fetches = [fetch] + [
+        pltpu.make_async_copy(a, b, ls.at[n_local + i])
+        for i, (a, b) in enumerate(((visc_in, visc), (absorb_in, absorb)))
+    ]
     stored = []
 
     def store(p0, np_, r0, nr):
@@ -93,9 +96,12 @@
         ps, rws = pl.ds(p0, np_), pl.ds(r0, nr)
         across.append([remote(source.at[ps, rws], buf.at[2 * k - 1, ps, rws], az_at(k)) for k in range(1, groups)])
         beside.append(remote(source.at[ps, rws], buf.at[0, ps, rws], sibling))
-        for c in across[-1] + [beside[-1]]:
+        for c in across[-1]:
             c.start()
             sent.append(c)
+    for c in beside:
+        c.start()
+        sent.append(c)
 
     def arrive(i):
         p0, np_, r0, nr = pieces[i]
@@ -215,8 +221,11 @@
 
         lax.fori_loop(p0, p0 + np_, one, 0)
 
+    for c in fetches:
+        c.start()
     arrive(0)
-    fetch.wait()
+    for c in fetches:
+        c.wait()
     for t in range(tiles):
         shift_tile(t, dust, 2)
     edges = [send_edge(s, dust, 2) for s in (0, 1)]
@@ -307,19 +316,22 @@
     n_tail = len(tail_planes(planes - 2))
     n_pieces = 1 + 2 + max(tiles - 3, 0) + n_tail
     n_scan = (n_rad - 1).bit_length()
+    n_local = 2 + max(tiles - 3, 0) + n_tail
     n_sems = n_pieces * (2 * (groups - 1) + 1) + 4 + n_scan
     f32 = jnp.float32
     vm = pl.BlockSpec(memory_space=pltpu.VMEM)
     hbm = pl.BlockSpec(memory_space=pl.ANY)
     moved, local = pl.pallas_call(
-        functools.partial(kernel, n_rad, n_az),
+        functools.partial(kernel, n_rad, n_az, n_local),
         out_shape=(
             jax.ShapeDtypeStruct((planes, rows, width), f32),
             jax.ShapeDtypeStruct((polar, rows, width), f32),
         ),
-        in_specs=[hbm, pl.BlockSpec(memory_space=pltpu.SMEM), vm, vm],
+        in_specs=[hbm, pl.BlockSpec(memory_space=pltpu.SMEM), hbm, hbm],
         out_specs=(hbm, vm),
         scratch_shapes=[
+            pltpu.VMEM((polar, rows, width), f32),
+            pltpu.VMEM((polar, rows, width), f32),
             pltpu.VMEM((polar, rows, width), f32),
             pltpu.VMEM((planes, rows, width), f32),
             pltpu.VMEM((planes, rows, width), f32),
@@ -331,7 +343,7 @@
             pltpu.VMEM((n_scan, polar, 1, width), f32),
             pltpu.SemaphoreType.DMA((n_sems,)),
             pltpu.SemaphoreType.DMA((n_sems,)),
-            pltpu.SemaphoreType.DMA((2 + max(tiles - 3, 0) + n_tail,)),
+            pltpu.SemaphoreType.DMA((n_local + 2,)),
         ],
         compiler_params=pltpu.CompilerParams(
             collective_id=0, has_side_effects=True, vmem_limit_bytes=56 * 2**20

time: 49.7 us -> 49.3 us (level)
  no operation moved by 1% of the time
where the time goes in v4:
time: 49.3 us; the launch traced here: 49.1 us
  Pallas kernels  45 us (91%)
  local copies, waits for them, and re-layouts  3.48 us (7%)
  between operations  0.65 us (1%)
    pallas_call x1, Pallas kernels, body(): pl.pallas_call(functools.partial(kernel, n_rad, n_az, n_local), out_shape...  45 us
    unnamed x4, local copies, waits for them, and re-layouts  3.48 us

profile of v4, /device:TPU:0, one launch (start us, length us, event | category | flops | bytes accessed | tf_op | source)
XLA Modules:
  0.0 49.1 jit_solution(13905562408317678621)
XLA Ops:
  0.6 45.0 %shard_map.59 = (f32[12,32,1024]{2,1,0:T(8,128)}, f32[2,32,1024]{2,1,0:T(8,128)}) custom-call(f32[12,32,1024]{2,1,0:T(8,128)} %bitcast.2, s32[32]{0:T(128)} %offs.1, f32[2,32,1024]{2,1,0:T(8,128)} %visc_in.1, f32[2,32,1024]{2,1,0:T(8,128)} %absorb_in.1), custom_call_target="tpu_custom_call" | custom-call | tf_op jit(solution)/shard_map/pallas_call | solution.py:324
  45.6 0.0 copy-start
  45.6 2.8 %copy.8 = f32[6,2,32,1024]{3,2,1,0:T(8,128)} copy(f32[6,2,32,1024]{3,2,1,0:T(8,128)} %bitcast.3) | data formatting | bytes 3145728
  48.4 0.0 copy-done
  48.4 0.7 %copy.9 = f32[2,32,1024]{2,1,0:T(8,128)} copy(f32[2,32,1024]{2,1,0:T(8,128)S(1)} %copy-done) | data formatting | bytes 524288
Async XLA Ops:
  45.6 2.8 %copy-start = (f32[2,32,1024]{2,1,0:T(8,128)S(1)}, f32[2,32,1024]{2,1,0:T(8,128)}, u32[]{:S(2)}) copy-start(f32[2,32,1024]{2,1,0:T(8,128)} %get-tuple-element.9) | copy-start | bytes 786436
